TPU v7x, 512 devices: a whole 4x8x8 slice. The times are simulated.
512 devices in a mesh: shot: 16 (over x_lo, z), tile: 32 (over y, x_hi, core).
Axes of the slice: x: 4 (x_hi: 2, x_lo: 2; x = x_hi * 2 + x_lo), y: 8, z: 8, core: 2. Of those that a mesh axis runs over, the one named last changes fastest.
Arguments:
- latent: bfloat16 [96, 16, 64, 64], P('tile', 'shot'), may hold values from -6 to 6
- kernel: bfloat16 [27, 64, 64], replicated, may hold values from -0.15625 to 0.15625
- conv_bias: float32 [64], replicated, may hold values from -3 to 3
- head_weight: bfloat16 [64], replicated, may hold values from -0.75 to 0.75
- density: float32 [192, 32, 128], P('tile'), may hold values from 1 to 2.5
- wave_prev: float32 [16, 192, 32, 128], P('shot', 'tile'), may hold values from -6 to 6
- wave_now: float32 [16, 192, 32, 128], P('shot', 'tile'), may hold values from -6 to 6
- adjoint_next: float32 [16, 192, 32, 128], P('shot', 'tile'), may hold values from -6 to 6
- adjoint_after: float32 [16, 192, 32, 128], P('shot', 'tile'), may hold values from -6 to 6
- source_cell: int32 [16], P('shot'), may hold values from 0 to 786431
- wavelet: float32 [16, 3], P('shot'), may hold values from -24 to 24
- receiver_cells: int32 [16, 128], P('shot'), may hold values from 0 to 786431
- observed: float32 [16, 3, 128], P('shot'), may hold values from -6 to 6
Outputs:
- latent_grad: float32 [96, 16, 64, 64], P('tile', 'shot')
- kernel_grad: float32 [27, 64, 64], replicated
- head_grad: float32 [64], replicated
- bias_grad: float32 [64], replicated
All inputs are finite; a program needn't handle non-finite values.
Results may differ from a plain program's by a relative error of at most 0.0034.
The roundings to bfloat16 on the way count: a program that leaves them out, or rounds other values in their place, can miss the bound.
Values may be sent and summed in bfloat16 or wider, within the bound.
No kernel may reach another device: no remote copies, remote signals or barrier semaphores. Data moves between devices by JAX's collectives and lax.ppermute only.
A program may use at most 64 MiB of HBM per device.

v0:
```python
import jax
import jax.numpy as jnp
from jax import lax
from jax.sharding import PartitionSpec as P

courant = 0.005
speed_low = 1.5
speed_span = 3.0


def padded_2(cells, sides, width):
    for axis, dim in sides:
        count = lax.axis_size(axis)
        ends = count - 1
        head = lax.slice_in_dim(cells, 0, width, axis=dim)
        tail = lax.slice_in_dim(cells, cells.shape[dim] - width, cells.shape[dim], axis=dim)
        cells = jnp.concatenate(
            [
                lax.ppermute(tail, axis, [(i, (i + 1) % count) for i in range(ends)]),
                cells,
                lax.ppermute(head, axis, [((i + 1) % count, i) for i in range(ends)]),
            ],
            axis=dim,
        )
    return cells


def upsample(coarse):
    coarse_x, coarse_z, channels, coarse_y = coarse.shape
    spread = jnp.broadcast_to(
        coarse[:, None, :, None, :, :, None], (coarse_x, 2, coarse_z, 2, channels, coarse_y, 2)
    )
    return spread.reshape(coarse_x * 2, coarse_z * 2, channels, coarse_y * 2)


def fold_children(fine):
    fine_x, fine_z, channels, fine_y = fine.shape
    grouped = fine.reshape(fine_x // 2, 2, fine_z // 2, 2, channels, fine_y // 2, 2)
    return jnp.sum(grouped, axis=(1, 3, 6))


def shifted_stack(padded, start_x, start_z, starts_y, cells_x, cells_z, cells_y):
    return jnp.concatenate(
        [
            padded[
                start_x : start_x + cells_x,
                start_z : start_z + cells_z,
                :,
                start_y : start_y + cells_y,
            ]
            for start_y in starts_y
        ],
        axis=2,
    )


def convolve(padded, kernel):
    cells_x = padded.shape[0] - 2
    cells_z = padded.shape[1] - 2
    channels = padded.shape[2]
    cells_y = padded.shape[3] - 2
    tap_table = kernel.reshape(3, 3, 3, channels, channels)
    result = jnp.zeros((cells_x, cells_z, channels, cells_y), jnp.float32)
    for offset_x in range(3):
        for offset_z in range(3):
            stacked = shifted_stack(
                padded, offset_x, offset_z, (0, 1, 2), cells_x, cells_z, cells_y
            )
            matrix = jnp.transpose(tap_table[offset_x, offset_z], (1, 0, 2)).reshape(
                channels, 3 * channels
            )
            result = result + jnp.einsum(
                "ok,abky->aboy", matrix, stacked, preferred_element_type=jnp.float32
            )
    return result


def kernel_terms(padded, grad_low):
    cells_x, cells_z, channels, cells_y = grad_low.shape
    pieces = []
    for offset_x in range(3):
        for offset_z in range(3):
            stacked = shifted_stack(
                padded, offset_x, offset_z, (0, 1, 2), cells_x, cells_z, cells_y
            )
            product = jnp.einsum(
                "aboy,abky->ok", grad_low, stacked, preferred_element_type=jnp.float32
            )
            pieces.append(jnp.transpose(product.reshape(channels, 3, channels), (1, 0, 2)))
    return jnp.stack(pieces).reshape(27, channels, channels)


def transposed(grad_padded, kernel):
    cells_x = grad_padded.shape[0] - 2
    cells_z = grad_padded.shape[1] - 2
    channels = grad_padded.shape[2]
    cells_y = grad_padded.shape[3] - 2
    tap_table = kernel.reshape(3, 3, 3, channels, channels)
    result = jnp.zeros((cells_x, cells_z, channels, cells_y), jnp.float32)
    for offset_x in range(3):
        for offset_z in range(3):
            stacked = shifted_stack(
                grad_padded, 2 - offset_x, 2 - offset_z, (2, 1, 0), cells_x, cells_z, cells_y
            )
            matrix = tap_table[offset_x, offset_z].reshape(3 * channels, channels)
            result = result + jnp.einsum(
                "kc,abky->abcy", matrix, stacked, preferred_element_type=jnp.float32
            )
    return result


def neighbours(padded):
    return (
        padded[2:, 1:-1, 1:-1],
        padded[:-2, 1:-1, 1:-1],
        padded[1:-1, 2:, 1:-1],
        padded[1:-1, :-2, 1:-1],
        padded[1:-1, 1:-1, 2:],
        padded[1:-1, 1:-1, :-2],
    )


def face_weights(padded_buoyancy):
    centre = padded_buoyancy[1:-1, 1:-1, 1:-1]
    return tuple((0.5 * (centre + beside) for beside in neighbours(padded_buoyancy)))


def apply_faces(padded, faces):
    centre = padded[1:-1, 1:-1, 1:-1]
    result = jnp.zeros_like(centre)
    for weight, beside in zip(faces, neighbours(padded)):
        result = result + weight * (beside - centre)
    return result


def propagate(
    laplace,
    coefficient,
    previous,
    current,
    following,
    beyond,
    anchor,
    source_cell,
    wavelet,
    receiver_cells,
    observed,
):
    field_shape = previous.shape
    field_cells = previous.size
    source_local = source_cell[0] - anchor
    source_owned = jnp.logical_and(source_local >= 0, source_local < field_cells).astype(
        jnp.float32
    )
    source_spot = jnp.clip(source_local, 0, field_cells - 1)
    receiver_local = receiver_cells[0] - anchor
    receiver_owned = jnp.logical_and(receiver_local >= 0, receiver_local < field_cells).astype(
        jnp.float32
    )
    receiver_spot = jnp.clip(receiver_local, 0, field_cells - 1)
    count_steps = wavelet.shape[1]
    laplacians = []
    residuals = []
    for instant in range(count_steps):
        laplacian = laplace(current)
        laplacians.append(laplacian)
        advanced = 2.0 * current - previous + coefficient * laplacian
        advanced = (
            advanced.reshape(-1)
            .at[source_spot]
            .add(source_owned * wavelet[0, instant])
            .reshape(field_shape)
        )
        residuals.append(
            receiver_owned * (advanced.reshape(-1)[receiver_spot] - observed[0, instant])
        )
        previous, current = (current, advanced)
    laplacians.append(laplace(current))
    coef_grad = following * laplacians[count_steps]
    for instant in reversed(range(count_steps)):
        preceding = 2.0 * following - beyond + laplace(coefficient * following)
        preceding = (
            preceding.reshape(-1).at[receiver_spot].add(residuals[instant]).reshape(field_shape)
        )
        coef_grad = coef_grad + preceding * laplacians[instant]
        beyond, following = (following, preceding)
    return coef_grad


def per_device(
    latent,
    kernel,
    conv_bias,
    head_weight,
    density,
    wave_prev,
    wave_now,
    adjoint_next,
    adjoint_after,
    source_cell,
    wavelet,
    receiver_cells,
    observed,
):
    extended = padded_2(upsample(latent), (("shot", 1), ("tile", 0)), 1)
    padded = jnp.pad(extended, ((0, 0), (0, 0), (0, 0), (1, 1)))
    pre_act = convolve(padded, kernel) + conv_bias[None, None, :, None]
    hidden = jax.nn.silu(pre_act).astype(jnp.bfloat16)
    logit = jnp.einsum("abcy,c->aby", hidden, head_weight, preferred_element_type=jnp.float32)
    squash = jax.nn.sigmoid(logit)
    velocity = speed_low + speed_span * squash
    tile_speed = lax.all_gather(velocity, "shot", axis=1, tiled=True)
    tile_cells = tile_speed.size
    buoyancy = 1.0 / density
    coefficient = courant * tile_speed * tile_speed * density
    factor = 2.0 * courant * tile_speed * density
    buoyancy_edges = padded_2(buoyancy, (("tile", 0),), 1)
    faces = face_weights(jnp.pad(buoyancy_edges, ((0, 0), (1, 1), (1, 1))))

    def laplace(field):
        field_edges = padded_2(field, (("tile", 0),), 1)
        return apply_faces(jnp.pad(field_edges, ((0, 0), (1, 1), (1, 1))), faces)

    anchor = lax.axis_index("tile") * tile_cells
    coef_grad = propagate(
        laplace,
        coefficient,
        wave_prev[0],
        wave_now[0],
        adjoint_next[0],
        adjoint_after[0],
        anchor,
        source_cell,
        wavelet,
        receiver_cells,
        observed,
    )
    strip_grad = lax.psum_scatter(coef_grad * factor, "shot", scatter_dimension=1, tiled=True)
    logit_grad = strip_grad * speed_span * squash * (1.0 - squash)
    head_part = jnp.einsum(
        "abcy,aby->c", hidden.astype(jnp.float32), logit_grad, precision=lax.Precision.HIGHEST
    )
    gate = jax.nn.sigmoid(pre_act)
    pre_grad = (
        logit_grad[:, :, None, :]
        * head_weight.astype(jnp.float32)[None, None, :, None]
        * (gate * (1.0 + pre_act * (1.0 - gate)))
    )
    bias_part = jnp.sum(pre_grad, axis=(0, 1, 3))
    grad_low = pre_grad.astype(jnp.bfloat16)
    kernel_part = kernel_terms(padded, grad_low)
    grad_edges = padded_2(grad_low, (("shot", 1), ("tile", 0)), 1)
    grad_padded = jnp.pad(grad_edges, ((0, 0), (0, 0), (0, 0), (1, 1)))
    latent_grad = fold_children(transposed(grad_padded, kernel))
    kernel_grad, head_grad, bias_grad = lax.psum(
        (kernel_part, head_part, bias_part), ("shot", "tile")
    )
    return (latent_grad, kernel_grad, head_grad, bias_grad)


def solution(mesh):
    return jax.shard_map(
        per_device,
        mesh=mesh,
        in_specs=(
            P("tile", "shot", None, None),
            P(),
            P(),
            P(),
            P("tile", None, None),
            P("shot", "tile", None, None),
            P("shot", "tile", None, None),
            P("shot", "tile", None, None),
            P("shot", "tile", None, None),
            P("shot"),
            P("shot", None),
            P("shot", None),
            P("shot", None, None),
        ),
        out_specs=(P("tile", "shot", None, None), P(), P(), P()),
        check_vma=False,
    )
```

profile of v0, /device:TPU:1, one launch (start us, length us, event | category | flops | bytes accessed | tf_op | source)
XLA Modules:
  0.0 589.9 jit_solution(18035886360403443610)
XLA Ops:
  8.4 4.8 collective-permute-start.1
  15.3 5.2 collective-permute-start.5
  20.5 2.2 collective-permute-start.7
  26.8 2.4 collective-permute-start.3
  29.2 1.9 collective-permute-start.4
  31.4 5.0 collective-permute-done.4
  42.4 32.4 %all_gather.3 = f32[6,32,128]{2,0,1:T(8,128)S(1)} all-gather(f32[6,2,128]{2,0,1:T(8,128)S(1)} %multiply_add_fusion.2), channel_id=1, replica_groups=mesh['shot'=16,'tile'=32] {'shot'}, dimensions={1}, use_global_device_ids=true | all-gather | bytes 104448 | tf_op jit(solution)/shard_map/all_gather | solution.py:212
  74.9 5.3 collective-permute-start
  80.3 6.1 %collective-permute-start.6 = (f32[1,32,128]{2,1,0:T(8,128)S(1)}, f32[1,32,128]{2,1,0:T(8,128)S(1)}, u32[]{:S(2)}, u32[]{:S(2)}) collective-permute-start(f32[1,32,128]{2,1,0:T(8,128)S(1)} %get-tuple-element.149), channel_id=1, source_target_pairs={{0,1},{1,2},{2,3},{3,4},{4,5},{5,6},{6,7},{7,8},{8,9},{9,10},{10,1... | collective-permute-start | bytes 49160 | tf_op jit(solution)/shard_map/ppermute | solution.py:19
  86.4 1.9 collective-permute-start.14
  88.4 5.1 collective-permute-start.15
  97.1 5.7 collective-permute-start.9
  106.1 5.7 collective-permute-start.11
  120.0 5.1 collective-permute-start.17
  127.1 5.1 collective-permute-start.13
  134.1 1.9 collective-permute-start.18
  136.0 5.5 collective-permute-start.19
  147.3 136.4 %all-reduce.17.cloned.1.call-done = f32[6,32,128]{2,1,0:T(8,128)} async-done(((f32[6,32,128]{2,1,0:T(8,128)}), f32[6,32,128]{2,1,0:T(8,128)}) %all-reduce.17.cloned.1.call-update) | async-done | bytes 98320
  297.0 2.1 collective-permute-done.21
  299.1 16.4 %collective-permute-start.22 = (bf16[1,4,64,128]{3,2,1,0:T(8,128)(2,1)S(1)}, bf16[1,4,64,128]{3,2,1,0:T(8,128)(2,1)S(1)}, u32[]{:S(2)}, u32[]{:S(2)}) collective-permute-start(bf16[1,4,64,128]{3,2,1,0:T(8,128)(2,1)S(1)} %get-tuple-element.129), channel_id=1, source_target_pairs={{0,1},{1,2},{2,3},{3,4},{4,5},{5,6},{6,7},{7,8},{8,9},{9,10},{10,1... | collective-permute-start | bytes 196616 | tf_op jit(solution)/shard_map/ppermute | solution.py:19
  315.5 1.9 collective-permute-start.23
  317.7 101.0 %all-reduce.11 = (f32[64]{0:T(128)}, f32[64]{0:T(128)}) all-reduce(f32[64]{0:T(128)S(1)} %convolution_bitcast_fusion, f32[64]{0:T(128)S(1)} %get-tuple-element.46), channel_id=1, replica_groups=mesh['shot'=16,'tile'=32] {'shot','tile'}, use_global_device_ids=true, to_apply=%region_7.8 | all-reduce | flops 128 | bytes 1024 | tf_op jit(solution)/shard_map/psum | solution.py:255
  426.6 154.3 %all-reduce.15.cloned.1.call-done = f32[27,64,64]{2,1,0:T(8,128)} async-done(((f32[27,64,64]{2,1,0:T(8,128)}), f32[27,64,64]{2,1,0:T(8,128)}) %all-reduce.15.cloned.1.call-update) | async-done | bytes 442384 | tf_op jit(solution)/shard_map/psum | solution.py:255
  580.9 2.2 copy.315
  (264 shorter events, 55.1 us)
Async XLA Ops:
  7.2 276.4 %all-reduce.17.cloned.1.call-start = ((), (), s32[]{:S(2)}) async-start(), calls=%async_computation.1 | async-start | bytes 196608
  8.4 18.3 %collective-permute-start.1 = (bf16[6,1,64,128]{3,2,1,0:T(8,128)(2,1)S(1)}, bf16[6,1,64,128]{3,2,1,0:T(8,128)(2,1)S(1)}, u32[]{:S(2)}, u32[]{:S(2)}) collective-permute-start(bf16[6,1,64,128]{3,2,1,0:T(8,128)(2,1)S(1)} %copy.176), channel_id=1, source_target_pairs={{0,32},{32,64},{64,96},{96,128},{128,160},{160,192},{192,224},{224... | collective-permute-start | bytes 294920 | tf_op jit(solution)/shard_map/ppermute | solution.py:19
  13.2 13.5 %collective-permute-start.2 = (bf16[6,1,64,128]{3,2,1,0:T(8,128)(2,1)S(1)}, bf16[6,1,64,128]{3,2,1,0:T(8,128)(2,1)S(1)}, u32[]{:S(2)}, u32[]{:S(2)}) collective-permute-start(bf16[6,1,64,128]{3,2,1,0:T(8,128)(2,1)S(1)} %copy.176), channel_id=1, source_target_pairs={{32,0},{64,32},{96,64},{128,96},{160,128},{192,160},{224,192},{256... | collective-permute-start | bytes 294920 | tf_op jit(solution)/shard_map/ppermute | solution.py:21
  15.3 15.9 %collective-permute-start.5 = (f32[1,32,128]{2,1,0:T(8,128)S(1)}, f32[1,32,128]{2,1,0:T(8,128)S(1)}, u32[]{:S(2)}, u32[]{:S(2)}) collective-permute-start(f32[1,32,128]{2,1,0:T(8,128)S(1)} %get-tuple-element.148), channel_id=1, source_target_pairs={{1,0},{2,1},{3,2},{4,3},{5,4},{6,5},{7,6},{8,7},{9,8},{10,9},{11,1... | collective-permute-start | bytes 49160 | tf_op jit(solution)/shard_map/ppermute | solution.py:21
  20.5 10.6 %collective-permute-start.7 = (f32[1,32,128]{2,1,0:T(8,128)S(1)}, f32[1,32,128]{2,1,0:T(8,128)S(1)}, u32[]{:S(2)}, u32[]{:S(2)}) collective-permute-start(f32[1,32,128]{2,1,0:T(8,128)S(1)} %get-tuple-element.147), channel_id=1, source_target_pairs={{0,1},{1,2},{2,3},{3,4},{4,5},{5,6},{6,7},{7,8},{8,9},{9,10},{10,1... | collective-permute-start | bytes 49160 | tf_op jit(solution)/shard_map/ppermute | solution.py:19
  29.2 7.1 %collective-permute-start.4 = (bf16[1,4,64,128]{3,2,1,0:T(8,128)(2,1)S(1)}, bf16[1,4,64,128]{3,2,1,0:T(8,128)(2,1)S(1)}, u32[]{:S(2)}, u32[]{:S(2)}) collective-permute-start(bf16[1,4,64,128]{3,2,1,0:T(8,128)(2,1)S(1)} %get-tuple-element.134), channel_id=1, source_target_pairs={{1,0},{2,1},{3,2},{4,3},{5,4},{6,5},{7,6},{8,7},{9,8},{10,9},{11,1... | collective-permute-start | bytes 196616 | tf_op jit(solution)/shard_map/ppermute | solution.py:21
  74.9 18.6 %collective-permute-start = (f32[1,32,128]{2,1,0:T(8,128)S(1)}, f32[1,32,128]{2,1,0:T(8,128)S(1)}, u32[]{:S(2)}, u32[]{:S(2)}) collective-permute-start(f32[1,32,128]{2,1,0:T(8,128)S(1)} %get-tuple-element.150), channel_id=1, source_target_pairs={{1,0},{2,1},{3,2},{4,3},{5,4},{6,5},{7,6},{8,7},{9,8},{10,9},{11,1... | collective-permute-start | bytes 49160 | tf_op jit(solution)/shard_map/ppermute | solution.py:21
  80.3 13.3 %collective-permute-start.6 = (f32[1,32,128]{2,1,0:T(8,128)S(1)}, f32[1,32,128]{2,1,0:T(8,128)S(1)}, u32[]{:S(2)}, u32[]{:S(2)}) collective-permute-start(f32[1,32,128]{2,1,0:T(8,128)S(1)} %get-tuple-element.149), channel_id=1, source_target_pairs={{0,1},{1,2},{2,3},{3,4},{4,5},{5,6},{6,7},{7,8},{8,9},{9,10},{10,1... | collective-permute-start | bytes 49160 | tf_op jit(solution)/shard_map/ppermute | solution.py:19
  86.4 7.3 %collective-permute-start.14 = (f32[1,32,128]{2,1,0:T(8,128)S(1)}, f32[1,32,128]{2,1,0:T(8,128)S(1)}, u32[]{:S(2)}, u32[]{:S(2)}) collective-permute-start(f32[1,32,128]{2,1,0:T(8,128)S(1)} %get-tuple-element.153), channel_id=1, source_target_pairs={{1,0},{2,1},{3,2},{4,3},{5,4},{6,5},{7,6},{8,7},{9,8},{10,9},{11,1... | collective-permute-start | bytes 49160 | tf_op jit(solution)/shard_map/ppermute | solution.py:21
  88.4 6.0 %collective-permute-start.15 = (f32[1,32,128]{2,1,0:T(8,128)S(1)}, f32[1,32,128]{2,1,0:T(8,128)S(1)}, u32[]{:S(2)}, u32[]{:S(2)}) collective-permute-start(f32[1,32,128]{2,1,0:T(8,128)S(1)} %get-tuple-element.152), channel_id=1, source_target_pairs={{0,1},{1,2},{2,3},{3,4},{4,5},{5,6},{6,7},{7,8},{8,9},{9,10},{10,1... | collective-permute-start | bytes 49160 | tf_op jit(solution)/shard_map/ppermute | solution.py:19
  95.2 8.3 %collective-permute-start.8 = (f32[1,32,128]{2,1,0:T(8,128)S(1)}, f32[1,32,128]{2,1,0:T(8,128)S(1)}, u32[]{:S(2)}, u32[]{:S(2)}) collective-permute-start(f32[1,32,128]{2,1,0:T(8,128)S(1)} %get-tuple-element.146), channel_id=1, source_target_pairs={{1,0},{2,1},{3,2},{4,3},{5,4},{6,5},{7,6},{8,7},{9,8},{10,9},{11,1... | collective-permute-start | bytes 49160 | tf_op jit(solution)/shard_map/ppermute | solution.py:21
  97.1 6.6 %collective-permute-start.9 = (f32[1,32,128]{2,1,0:T(8,128)S(1)}, f32[1,32,128]{2,1,0:T(8,128)S(1)}, u32[]{:S(2)}, u32[]{:S(2)}) collective-permute-start(f32[1,32,128]{2,1,0:T(8,128)S(1)} %get-tuple-element.145), channel_id=1, source_target_pairs={{0,1},{1,2},{2,3},{3,4},{4,5},{5,6},{6,7},{7,8},{8,9},{9,10},{10,1... | collective-permute-start | bytes 49160 | tf_op jit(solution)/shard_map/ppermute | solution.py:19
  104.2 10.6 %collective-permute-start.10 = (f32[1,32,128]{2,1,0:T(8,128)S(1)}, f32[1,32,128]{2,1,0:T(8,128)S(1)}, u32[]{:S(2)}, u32[]{:S(2)}) collective-permute-start(f32[1,32,128]{2,1,0:T(8,128)S(1)} %get-tuple-element.144), channel_id=1, source_target_pairs={{1,0},{2,1},{3,2},{4,3},{5,4},{6,5},{7,6},{8,7},{9,8},{10,9},{11,1... | collective-permute-start | bytes 49160 | tf_op jit(solution)/shard_map/ppermute | solution.py:21
  106.1 8.7 %collective-permute-start.11 = (f32[1,32,128]{2,1,0:T(8,128)S(1)}, f32[1,32,128]{2,1,0:T(8,128)S(1)}, u32[]{:S(2)}, u32[]{:S(2)}) collective-permute-start(f32[1,32,128]{2,1,0:T(8,128)S(1)} %get-tuple-element.143), channel_id=1, source_target_pairs={{0,1},{1,2},{2,3},{3,4},{4,5},{5,6},{6,7},{7,8},{8,9},{9,10},{10,1... | collective-permute-start | bytes 49160 | tf_op jit(solution)/shard_map/ppermute | solution.py:19
  118.1 14.2 %collective-permute-start.16 = (f32[1,32,128]{2,1,0:T(8,128)S(1)}, f32[1,32,128]{2,1,0:T(8,128)S(1)}, u32[]{:S(2)}, u32[]{:S(2)}) collective-permute-start(f32[1,32,128]{2,1,0:T(8,128)S(1)} %get-tuple-element.140), channel_id=1, source_target_pairs={{1,0},{2,1},{3,2},{4,3},{5,4},{6,5},{7,6},{8,7},{9,8},{10,9},{11,1... | collective-permute-start | bytes 49160 | tf_op jit(solution)/shard_map/ppermute | solution.py:21
  120.0 12.3 %collective-permute-start.17 = (f32[1,32,128]{2,1,0:T(8,128)S(1)}, f32[1,32,128]{2,1,0:T(8,128)S(1)}, u32[]{:S(2)}, u32[]{:S(2)}) collective-permute-start(f32[1,32,128]{2,1,0:T(8,128)S(1)} %get-tuple-element.139), channel_id=1, source_target_pairs={{0,1},{1,2},{2,3},{3,4},{4,5},{5,6},{6,7},{7,8},{8,9},{9,10},{10,1... | collective-permute-start | bytes 49160 | tf_op jit(solution)/shard_map/ppermute | solution.py:19
  125.2 16.4 %collective-permute-start.12 = (f32[1,32,128]{2,1,0:T(8,128)S(1)}, f32[1,32,128]{2,1,0:T(8,128)S(1)}, u32[]{:S(2)}, u32[]{:S(2)}) collective-permute-start(f32[1,32,128]{2,1,0:T(8,128)S(1)} %get-tuple-element.142), channel_id=1, source_target_pairs={{1,0},{2,1},{3,2},{4,3},{5,4},{6,5},{7,6},{8,7},{9,8},{10,9},{11,1... | collective-permute-start | bytes 49160 | tf_op jit(solution)/shard_map/ppermute | solution.py:21
  127.1 14.5 %collective-permute-start.13 = (f32[1,32,128]{2,1,0:T(8,128)S(1)}, f32[1,32,128]{2,1,0:T(8,128)S(1)}, u32[]{:S(2)}, u32[]{:S(2)}) collective-permute-start(f32[1,32,128]{2,1,0:T(8,128)S(1)} %get-tuple-element.141), channel_id=1, source_target_pairs={{0,1},{1,2},{2,3},{3,4},{4,5},{5,6},{6,7},{7,8},{8,9},{9,10},{10,1... | collective-permute-start | bytes 49160 | tf_op jit(solution)/shard_map/ppermute | solution.py:19
  134.1 7.6 %collective-permute-start.18 = (f32[1,32,128]{2,1,0:T(8,128)S(1)}, f32[1,32,128]{2,1,0:T(8,128)S(1)}, u32[]{:S(2)}, u32[]{:S(2)}) collective-permute-start(f32[1,32,128]{2,1,0:T(8,128)S(1)} %get-tuple-element.138), channel_id=1, source_target_pairs={{1,0},{2,1},{3,2},{4,3},{5,4},{6,5},{7,6},{8,7},{9,8},{10,9},{11,1... | collective-permute-start | bytes 49160 | tf_op jit(solution)/shard_map/ppermute | solution.py:21
  136.0 6.4 %collective-permute-start.19 = (f32[1,32,128]{2,1,0:T(8,128)S(1)}, f32[1,32,128]{2,1,0:T(8,128)S(1)}, u32[]{:S(2)}, u32[]{:S(2)}) collective-permute-start(f32[1,32,128]{2,1,0:T(8,128)S(1)} %get-tuple-element.137), channel_id=1, source_target_pairs={{0,1},{1,2},{2,3},{3,4},{4,5},{5,6},{6,7},{7,8},{8,9},{9,10},{10,1... | collective-permute-start | bytes 49160 | tf_op jit(solution)/shard_map/ppermute | solution.py:19
  145.3 435.6 %all-reduce.15.cloned.1.call-start = ((), (), s32[]{:S(2)}) async-start(), calls=%async_computation | async-start | bytes 1769472 | tf_op jit(solution)/shard_map/psum | solution.py:255
  293.7 5.4 collective-permute-start.21
  299.1 119.6 %collective-permute-start.22 = (bf16[1,4,64,128]{3,2,1,0:T(8,128)(2,1)S(1)}, bf16[1,4,64,128]{3,2,1,0:T(8,128)(2,1)S(1)}, u32[]{:S(2)}, u32[]{:S(2)}) collective-permute-start(bf16[1,4,64,128]{3,2,1,0:T(8,128)(2,1)S(1)} %get-tuple-element.129), channel_id=1, source_target_pairs={{0,1},{1,2},{2,3},{3,4},{4,5},{5,6},{6,7},{7,8},{8,9},{9,10},{10,1... | collective-permute-start | bytes 196616 | tf_op jit(solution)/shard_map/ppermute | solution.py:19
  315.5 103.2 %collective-permute-start.23 = (bf16[1,4,64,128]{3,2,1,0:T(8,128)(2,1)S(1)}, bf16[1,4,64,128]{3,2,1,0:T(8,128)(2,1)S(1)}, u32[]{:S(2)}, u32[]{:S(2)}) collective-permute-start(bf16[1,4,64,128]{3,2,1,0:T(8,128)(2,1)S(1)} %get-tuple-element.130), channel_id=1, source_target_pairs={{1,0},{2,1},{3,2},{4,3},{5,4},{6,5},{7,6},{8,7},{9,8},{10,9},{11,1... | collective-permute-start | bytes 196616 | tf_op jit(solution)/shard_map/ppermute | solution.py:21
  (60 other events, 304.2 us)
Sparse Core Ops, SparseCore 0:
  145.4 138.1 all-reduce.16
  297.1 283.7 all-reduce.14
where the time goes:
time: 591 us; the launch traced here: 590 us
  waiting for transfers between devices  299 us (51%)
  blocking collectives  133 us (23%)
  starting transfers between devices  94.6 us (16%)
  local copies, waits for them, and re-layouts  24.3 us (4%)
  between operations  18.9 us (3%)
  other arithmetic  10.4 us (2%)
  matrix products  9.01 us (2%)
    psum x1, waiting for transfers between devices, per_device(): lax.psum((kernel_part, head_part, bias_part), ('shot', 'tile'))  154 us
    unnamed x3, waiting for transfers between devices  136 us
    psum x1, blocking collectives, per_device(): lax.psum((kernel_part, head_part, bias_part), ('shot', 'tile'))  101 us
    ppermute x12, starting transfers between devices, padded_2(): lax.ppermute(tail, axis, [(i, (i + 1) % count) for i in range(ends)])  66 us
    all_gather x1, blocking collectives, per_device(): tile_speed = lax.all_gather(velocity, 'shot', axis=1, tiled=True)  32.4 us
    ppermute x12, starting transfers between devices, padded_2(): lax.ppermute(head, axis, [((i + 1) % count, i) for i in range(ends)])  28.5 us
    unnamed x128, local copies, waits for them, and re-layouts  12.5 us
  transfers between devices with their start and end apart: 26, of which 7 were waited for; matrix products, arithmetic and copies ran while one was open for 3% of the time, Pallas kernels for 0%

commit v1 on v0

--- a/solution.py
+++ b/solution.py
@@ -1,3 +1,4 @@
+import functools
 import jax
 import jax.numpy as jnp
 from jax import lax
@@ -6,6 +7,15 @@
 courant = 0.005
 speed_low = 1.5
 speed_span = 3.0
+
+
+def read_arrays(u, net_axis, ax_name):
+    for rr in (net_axis, ax_name):
+        u = lax.psum(u, axis_name=rr)
+    return u
+
+
+do_the_edge = functools.partial(read_arrays, net_axis="tile", ax_name="shot")
 
 
 def padded_2(cells, sides, width):
@@ -252,9 +262,7 @@
     grad_edges = padded_2(grad_low, (("shot", 1), ("tile", 0)), 1)
     grad_padded = jnp.pad(grad_edges, ((0, 0), (0, 0), (0, 0), (1, 1)))
     latent_grad = fold_children(transposed(grad_padded, kernel))
-    kernel_grad, head_grad, bias_grad = lax.psum(
-        (kernel_part, head_part, bias_part), ("shot", "tile")
-    )
+    kernel_grad, head_grad, bias_grad = do_the_edge((kernel_part, head_part, bias_part))
     return (latent_grad, kernel_grad, head_grad, bias_grad)
 
 

time: 591 us -> 733 us (1.24); the launches traced: 590 us -> 721 us
  waiting for transfers between devices: 299 us -> 440 us
  blocking collectives: 133 us -> 125 us
    psum x1 -> x2, waiting for transfers between devices: 154 us -> 295 us  [read_arrays(): u = lax.psum(u, axis_name=rr)]
    psum x1 -> x2, blocking collectives: 101 us -> 92.2 us  [read_arrays(): u = lax.psum(u, axis_name=rr)]
    unnamed x3 -> x4, waiting for transfers between devices: 136 us -> 136 us
  transfers between devices with their start and end apart: 26 -> 27, of which waited for: 7 -> 8; matrix products, arithmetic and copies ran while one was open for 3% -> 2% of each run, Pallas kernels for 0% -> 0%
where the time goes in v1:
time: 733 us; the launch traced here: 721 us
  waiting for transfers between devices  440 us (60%)
  blocking collectives  125 us (17%)
  starting transfers between devices  94.6 us (13%)
  local copies, waits for them, and re-layouts  24.5 us (3%)
  between operations  18.7 us (3%)
  other arithmetic  10.4 us (1%)
  matrix products  9.01 us (1%)
    psum x2, waiting for transfers between devices, read_arrays(): u = lax.psum(u, axis_name=rr)  295 us
    unnamed x4, waiting for transfers between devices  136 us
    psum x2, blocking collectives, read_arrays(): u = lax.psum(u, axis_name=rr)  92.2 us
    ppermute x12, starting transfers between devices, padded_2(): lax.ppermute(tail, axis, [(i, (i + 1) % count) for i in range(ends)])  66 us
    all_gather x1, blocking collectives, per_device(): tile_speed = lax.all_gather(velocity, 'shot', axis=1, tiled=True)  32.4 us
    ppermute x12, starting transfers between devices, padded_2(): lax.ppermute(head, axis, [((i + 1) % count, i) for i in range(ends)])  28.5 us
  transfers between devices with their start and end apart: 27, of which 8 were waited for; matrix products, arithmetic and copies ran while one was open for 2% of the time, Pallas kernels for 0%

profile of v1, /device:TPU:1, one launch (start us, length us, event | category | flops | bytes accessed | tf_op | source)
XLA Modules:
  0.0 721.4 jit_solution(797878365370146137)
XLA Ops:
  8.4 4.8 collective-permute-start.1
  15.3 5.2 collective-permute-start.5
  20.5 2.2 collective-permute-start.7
  26.8 2.4 collective-permute-start.3
  29.2 1.9 collective-permute-start.4
  31.4 5.0 collective-permute-done.4
  42.4 32.4 %all_gather.3 = f32[6,32,128]{2,0,1:T(8,128)S(1)} all-gather(f32[6,2,128]{2,0,1:T(8,128)S(1)} %multiply_add_fusion.2), channel_id=1, replica_groups=mesh['shot'=16,'tile'=32] {'shot'}, dimensions={1}, use_global_device_ids=true | all-gather | bytes 104448 | tf_op jit(solution)/shard_map/all_gather | solution.py:222
  74.9 5.3 collective-permute-start
  80.2 6.1 collective-permute-start.6
  86.4 1.9 collective-permute-start.14
  88.3 5.1 collective-permute-start.15
  97.1 5.7 collective-permute-start.9
  106.1 5.7 collective-permute-start.11
  120.0 5.1 collective-permute-start.17
  127.0 5.1 collective-permute-start.13
  136.0 5.5 collective-permute-start.19
  147.2 136.4 %all-reduce.21.cloned.1.call-done = f32[6,32,128]{2,1,0:T(8,128)} async-done(((f32[6,32,128]{2,1,0:T(8,128)}), f32[6,32,128]{2,1,0:T(8,128)}) %all-reduce.21.cloned.1.call-update) | async-done | bytes 98320
  297.0 2.0 collective-permute-done.21
  299.0 16.4 %collective-permute-start.22 = (bf16[1,4,64,128]{3,2,1,0:T(8,128)(2,1)S(1)}, bf16[1,4,64,128]{3,2,1,0:T(8,128)(2,1)S(1)}, u32[]{:S(2)}, u32[]{:S(2)}) collective-permute-start(bf16[1,4,64,128]{3,2,1,0:T(8,128)(2,1)S(1)} %get-tuple-element.131), channel_id=1, source_target_pairs={{0,1},{1,2},{2,3},{3,4},{4,5},{5,6},{6,7},{7,8},{8,9},{9,10},{10,1... | collective-permute-start | bytes 196616 | tf_op jit(solution)/shard_map/ppermute | solution.py:29
  317.6 65.1 %all-reduce.11 = (f32[64]{0:T(128)S(1)}, f32[64]{0:T(128)S(1)}) all-reduce(f32[64]{0:T(128)S(1)} %convolution_bitcast_fusion, f32[64]{0:T(128)S(1)} %get-tuple-element.48), channel_id=1, replica_groups=mesh['shot'=16,'tile'=32] {'tile'}, use_global_device_ids=true, to_apply=%region_8.9 | all-reduce | flops 128 | bytes 1024 | tf_op jit(solution)/shard_map/psum | solution.py:14
  382.7 27.1 %all-reduce.12 = (f32[64]{0:T(128)}, f32[64]{0:T(128)}) all-reduce(f32[64]{0:T(128)S(1)} %get-tuple-element.44, f32[64]{0:T(128)S(1)} %get-tuple-element.45), channel_id=1, replica_groups=mesh['shot'=16,'tile'=32] {'shot'}, use_global_device_ids=true, to_apply=%region_9.10 | all-reduce | flops 128 | bytes 1024 | tf_op jit(solution)/shard_map/psum | solution.py:14
  415.4 161.3 %all-reduce.17.cloned.1.call-done = f32[27,64,64]{2,1,0:T(8,128)} async-done(((f32[27,64,64]{2,1,0:T(8,128)}), f32[27,64,64]{2,1,0:T(8,128)}) %all-reduce.17.cloned.1.call-update) | async-done | bytes 442384 | tf_op jit(solution)/shard_map/psum | solution.py:14
  579.3 133.3 %all-reduce.19.cloned.1.call-done = f32[27,64,64]{2,1,0:T(8,128)} async-done(((f32[27,64,64]{2,1,0:T(8,128)}), f32[27,64,64]{2,1,0:T(8,128)}) %all-reduce.19.cloned.1.call-update) | async-done | bytes 442384 | tf_op jit(solution)/shard_map/psum | solution.py:14
  712.7 2.2 copy.316
  (268 shorter events, 59.1 us)
Async XLA Ops:
  7.2 276.4 %all-reduce.21.cloned.1.call-start = ((), (), s32[]{:S(2)}) async-start(), calls=%async_computation.2 | async-start | bytes 196608
  8.4 18.3 %collective-permute-start.1 = (bf16[6,1,64,128]{3,2,1,0:T(8,128)(2,1)S(1)}, bf16[6,1,64,128]{3,2,1,0:T(8,128)(2,1)S(1)}, u32[]{:S(2)}, u32[]{:S(2)}) collective-permute-start(bf16[6,1,64,128]{3,2,1,0:T(8,128)(2,1)S(1)} %copy.176), channel_id=1, source_target_pairs={{0,32},{32,64},{64,96},{96,128},{128,160},{160,192},{192,224},{224... | collective-permute-start | bytes 294920 | tf_op jit(solution)/shard_map/ppermute | solution.py:29
  13.3 13.5 %collective-permute-start.2 = (bf16[6,1,64,128]{3,2,1,0:T(8,128)(2,1)S(1)}, bf16[6,1,64,128]{3,2,1,0:T(8,128)(2,1)S(1)}, u32[]{:S(2)}, u32[]{:S(2)}) collective-permute-start(bf16[6,1,64,128]{3,2,1,0:T(8,128)(2,1)S(1)} %copy.176), channel_id=1, source_target_pairs={{32,0},{64,32},{96,64},{128,96},{160,128},{192,160},{224,192},{256... | collective-permute-start | bytes 294920 | tf_op jit(solution)/shard_map/ppermute | solution.py:31
  15.3 15.9 %collective-permute-start.5 = (f32[1,32,128]{2,1,0:T(8,128)S(1)}, f32[1,32,128]{2,1,0:T(8,128)S(1)}, u32[]{:S(2)}, u32[]{:S(2)}) collective-permute-start(f32[1,32,128]{2,1,0:T(8,128)S(1)} %get-tuple-element.150), channel_id=1, source_target_pairs={{1,0},{2,1},{3,2},{4,3},{5,4},{6,5},{7,6},{8,7},{9,8},{10,9},{11,1... | collective-permute-start | bytes 49160 | tf_op jit(solution)/shard_map/ppermute | solution.py:31
  20.5 10.6 %collective-permute-start.7 = (f32[1,32,128]{2,1,0:T(8,128)S(1)}, f32[1,32,128]{2,1,0:T(8,128)S(1)}, u32[]{:S(2)}, u32[]{:S(2)}) collective-permute-start(f32[1,32,128]{2,1,0:T(8,128)S(1)} %get-tuple-element.149), channel_id=1, source_target_pairs={{0,1},{1,2},{2,3},{3,4},{4,5},{5,6},{6,7},{7,8},{8,9},{9,10},{10,1... | collective-permute-start | bytes 49160 | tf_op jit(solution)/shard_map/ppermute | solution.py:29
  29.2 7.1 collective-permute-start.4
  74.9 18.6 %collective-permute-start = (f32[1,32,128]{2,1,0:T(8,128)S(1)}, f32[1,32,128]{2,1,0:T(8,128)S(1)}, u32[]{:S(2)}, u32[]{:S(2)}) collective-permute-start(f32[1,32,128]{2,1,0:T(8,128)S(1)} %get-tuple-element.152), channel_id=1, source_target_pairs={{1,0},{2,1},{3,2},{4,3},{5,4},{6,5},{7,6},{8,7},{9,8},{10,9},{11,1... | collective-permute-start | bytes 49160 | tf_op jit(solution)/shard_map/ppermute | solution.py:31
  80.2 13.3 %collective-permute-start.6 = (f32[1,32,128]{2,1,0:T(8,128)S(1)}, f32[1,32,128]{2,1,0:T(8,128)S(1)}, u32[]{:S(2)}, u32[]{:S(2)}) collective-permute-start(f32[1,32,128]{2,1,0:T(8,128)S(1)} %get-tuple-element.151), channel_id=1, source_target_pairs={{0,1},{1,2},{2,3},{3,4},{4,5},{5,6},{6,7},{7,8},{8,9},{9,10},{10,1... | collective-permute-start | bytes 49160 | tf_op jit(solution)/shard_map/ppermute | solution.py:29
  86.4 7.3 %collective-permute-start.14 = (f32[1,32,128]{2,1,0:T(8,128)S(1)}, f32[1,32,128]{2,1,0:T(8,128)S(1)}, u32[]{:S(2)}, u32[]{:S(2)}) collective-permute-start(f32[1,32,128]{2,1,0:T(8,128)S(1)} %get-tuple-element.155), channel_id=1, source_target_pairs={{1,0},{2,1},{3,2},{4,3},{5,4},{6,5},{7,6},{8,7},{9,8},{10,9},{11,1... | collective-permute-start | bytes 49160 | tf_op jit(solution)/shard_map/ppermute | solution.py:31
  88.3 6.0 collective-permute-start.15
  95.1 8.4 %collective-permute-start.8 = (f32[1,32,128]{2,1,0:T(8,128)S(1)}, f32[1,32,128]{2,1,0:T(8,128)S(1)}, u32[]{:S(2)}, u32[]{:S(2)}) collective-permute-start(f32[1,32,128]{2,1,0:T(8,128)S(1)} %get-tuple-element.148), channel_id=1, source_target_pairs={{1,0},{2,1},{3,2},{4,3},{5,4},{6,5},{7,6},{8,7},{9,8},{10,9},{11,1... | collective-permute-start | bytes 49160 | tf_op jit(solution)/shard_map/ppermute | solution.py:31
  97.1 6.6 collective-permute-start.9
  104.2 10.6 %collective-permute-start.10 = (f32[1,32,128]{2,1,0:T(8,128)S(1)}, f32[1,32,128]{2,1,0:T(8,128)S(1)}, u32[]{:S(2)}, u32[]{:S(2)}) collective-permute-start(f32[1,32,128]{2,1,0:T(8,128)S(1)} %get-tuple-element.146), channel_id=1, source_target_pairs={{1,0},{2,1},{3,2},{4,3},{5,4},{6,5},{7,6},{8,7},{9,8},{10,9},{11,1... | collective-permute-start | bytes 49160 | tf_op jit(solution)/shard_map/ppermute | solution.py:31
  106.1 8.7 %collective-permute-start.11 = (f32[1,32,128]{2,1,0:T(8,128)S(1)}, f32[1,32,128]{2,1,0:T(8,128)S(1)}, u32[]{:S(2)}, u32[]{:S(2)}) collective-permute-start(f32[1,32,128]{2,1,0:T(8,128)S(1)} %get-tuple-element.145), channel_id=1, source_target_pairs={{0,1},{1,2},{2,3},{3,4},{4,5},{5,6},{6,7},{7,8},{8,9},{9,10},{10,1... | collective-permute-start | bytes 49160 | tf_op jit(solution)/shard_map/ppermute | solution.py:29
  118.0 14.2 %collective-permute-start.16 = (f32[1,32,128]{2,1,0:T(8,128)S(1)}, f32[1,32,128]{2,1,0:T(8,128)S(1)}, u32[]{:S(2)}, u32[]{:S(2)}) collective-permute-start(f32[1,32,128]{2,1,0:T(8,128)S(1)} %get-tuple-element.142), channel_id=1, source_target_pairs={{1,0},{2,1},{3,2},{4,3},{5,4},{6,5},{7,6},{8,7},{9,8},{10,9},{11,1... | collective-permute-start | bytes 49160 | tf_op jit(solution)/shard_map/ppermute | solution.py:31
  120.0 12.3 %collective-permute-start.17 = (f32[1,32,128]{2,1,0:T(8,128)S(1)}, f32[1,32,128]{2,1,0:T(8,128)S(1)}, u32[]{:S(2)}, u32[]{:S(2)}) collective-permute-start(f32[1,32,128]{2,1,0:T(8,128)S(1)} %get-tuple-element.141), channel_id=1, source_target_pairs={{0,1},{1,2},{2,3},{3,4},{4,5},{5,6},{6,7},{7,8},{8,9},{9,10},{10,1... | collective-permute-start | bytes 49160 | tf_op jit(solution)/shard_map/ppermute | solution.py:29
  125.1 16.4 %collective-permute-start.12 = (f32[1,32,128]{2,1,0:T(8,128)S(1)}, f32[1,32,128]{2,1,0:T(8,128)S(1)}, u32[]{:S(2)}, u32[]{:S(2)}) collective-permute-start(f32[1,32,128]{2,1,0:T(8,128)S(1)} %get-tuple-element.144), channel_id=1, source_target_pairs={{1,0},{2,1},{3,2},{4,3},{5,4},{6,5},{7,6},{8,7},{9,8},{10,9},{11,1... | collective-permute-start | bytes 49160 | tf_op jit(solution)/shard_map/ppermute | solution.py:31
  127.0 14.5 %collective-permute-start.13 = (f32[1,32,128]{2,1,0:T(8,128)S(1)}, f32[1,32,128]{2,1,0:T(8,128)S(1)}, u32[]{:S(2)}, u32[]{:S(2)}) collective-permute-start(f32[1,32,128]{2,1,0:T(8,128)S(1)} %get-tuple-element.143), channel_id=1, source_target_pairs={{0,1},{1,2},{2,3},{3,4},{4,5},{5,6},{6,7},{7,8},{8,9},{9,10},{10,1... | collective-permute-start | bytes 49160 | tf_op jit(solution)/shard_map/ppermute | solution.py:29
  134.1 7.6 %collective-permute-start.18 = (f32[1,32,128]{2,1,0:T(8,128)S(1)}, f32[1,32,128]{2,1,0:T(8,128)S(1)}, u32[]{:S(2)}, u32[]{:S(2)}) collective-permute-start(f32[1,32,128]{2,1,0:T(8,128)S(1)} %get-tuple-element.140), channel_id=1, source_target_pairs={{1,0},{2,1},{3,2},{4,3},{5,4},{6,5},{7,6},{8,7},{9,8},{10,9},{11,1... | collective-permute-start | bytes 49160 | tf_op jit(solution)/shard_map/ppermute | solution.py:31
  136.0 6.4 collective-permute-start.19
  145.2 431.5 %all-reduce.17.cloned.1.call-start = ((), (), s32[]{:S(2)}) async-start(), calls=%async_computation | async-start | bytes 1769472 | tf_op jit(solution)/shard_map/psum | solution.py:14
  296.9 415.7 %all-reduce.19.cloned.1.call-start = ((), (), s32[]{:S(2)}) async-start(), calls=%async_computation.1 | async-start | bytes 1769472 | tf_op jit(solution)/shard_map/psum | solution.py:14
  299.0 110.8 %collective-permute-start.22 = (bf16[1,4,64,128]{3,2,1,0:T(8,128)(2,1)S(1)}, bf16[1,4,64,128]{3,2,1,0:T(8,128)(2,1)S(1)}, u32[]{:S(2)}, u32[]{:S(2)}) collective-permute-start(bf16[1,4,64,128]{3,2,1,0:T(8,128)(2,1)S(1)} %get-tuple-element.131), channel_id=1, source_target_pairs={{0,1},{1,2},{2,3},{3,4},{4,5},{5,6},{6,7},{7,8},{8,9},{9,10},{10,1... | collective-permute-start | bytes 196616 | tf_op jit(solution)/shard_map/ppermute | solution.py:29
  315.5 94.4 %collective-permute-start.23 = (bf16[1,4,64,128]{3,2,1,0:T(8,128)(2,1)S(1)}, bf16[1,4,64,128]{3,2,1,0:T(8,128)(2,1)S(1)}, u32[]{:S(2)}, u32[]{:S(2)}) collective-permute-start(bf16[1,4,64,128]{3,2,1,0:T(8,128)(2,1)S(1)} %get-tuple-element.132), channel_id=1, source_target_pairs={{1,0},{2,1},{3,2},{4,3},{5,4},{6,5},{7,6},{8,7},{9,8},{10,9},{11,1... | collective-permute-start | bytes 196616 | tf_op jit(solution)/shard_map/ppermute | solution.py:31
  (61 other events, 470.1 us)
Sparse Core Ops, SparseCore 0:
  145.3 138.1 all-reduce.20
  297.1 279.6 all-reduce.16
  579.7 132.9 all-reduce.18
